TPU v7x, 32 devices: a whole 2x2x4 slice. The times are simulated.
32 devices in a mesh: freq: 8 (over z, x), row: 4 (over y, core).
Axes of the slice: x: 2, y: 2, z: 4, core: 2. Of those that a mesh axis runs over, the one named last changes fastest.
Arguments:
- operator: bfloat16 [8, 1024, 2, 1024], P('freq', 'row'), may hold values from -0.125 to 0.125
- recorded: bfloat16 [8, 1024, 2, 512], P('freq', 'row'), may hold values from -6 to 6
- filter_coefficients: float32 [3, 8, 1024], P(None, None, ('row', 'freq')), may hold values from -1.2 to 1.2
- tap_delays: int32 [8], replicated, may hold values from 0 to 63, as said below
Outputs:
- primaries: bfloat16 [1024, 512, 1024], P(('row', 'freq'))
Inputs may be any that keep to these rules, and one draw needn't show every extreme that they name: `tap_delays`: the delays are not distinct in general; at least one tap has delay 64 - 1.
All inputs are finite; a program needn't handle non-finite values.
Results may differ from a plain program's by a relative error of at most 0.008.
Values may be sent and summed in bfloat16 or wider, within the bound.
A program may use at most 192 MiB of HBM per device.

v0:
```python
import math

import jax
import jax.numpy as jnp
from jax import lax
from jax.sharding import PartitionSpec as P

NT = 1024
MAXLAG = 64


shrink_level = 0.5


def padded_2(block, sides, width):
    for axis, dim in sides:
        count = lax.axis_size(axis)
        forward = [(i, i + 1) for i in range(count - 1)]
        backward = [(target, source) for source, target in forward]
        low = lax.ppermute(
            lax.slice_in_dim(block, block.shape[dim] - width, None, axis=dim), axis, forward
        )
        high = lax.ppermute(lax.slice_in_dim(block, 0, width, axis=dim), axis, backward)
        block = jnp.concatenate([low, block, high], axis=dim)
    return block


def inverse_lookup(harmonics, time_step_total):
    overtone_indices = jnp.arange(harmonics) + 1
    recording_epochs = jnp.arange(time_step_total)
    rotation_radians = (
        overtone_indices[:, None] * recording_epochs[None, :] % time_step_total
    ).astype(jnp.float32) * (2.0 * math.pi / time_step_total)
    scale = 1.0 / math.sqrt(harmonics)
    return jnp.stack(
        [jnp.cos(rotation_radians) * scale, -jnp.sin(rotation_radians) * scale], axis=1
    ).astype(jnp.bfloat16)


def complex_block(columns, segment):
    real_component = segment[:, 0]
    imag_part = segment[:, 1]
    upper = jnp.concatenate([real_component, imag_part], axis=1)
    lower = jnp.concatenate([-imag_part, real_component], axis=1)
    return jnp.dot(
        columns, jnp.concatenate([upper, lower], axis=0), preferred_element_type=jnp.float32
    )


def match_filter(border_rows, weights, tap_delays, row_count, time_step_total):
    padded = jnp.pad(border_rows, ((0, 0), (0, 0), (MAXLAG, 0)))
    estimate = jnp.zeros((row_count, border_rows.shape[1], time_step_total), jnp.float32)
    anchor = jnp.zeros((), jnp.int32)
    for tap_index in range(weights.shape[1]):
        begin = MAXLAG - tap_delays[tap_index]
        displaced_trace = lax.dynamic_slice(
            padded, (anchor, anchor, begin), (padded.shape[0], padded.shape[1], time_step_total)
        )
        for neighbour in range(3):
            factor = weights[neighbour, tap_index][:, None, None]
            estimate = estimate + factor * displaced_trace[
                neighbour : neighbour + row_count
            ].astype(jnp.float32)
    return estimate


def shrink(data_time, estimate):
    residual = data_time.astype(jnp.float32) - estimate
    return (jnp.sign(residual) * jnp.maximum(jnp.abs(residual) - shrink_level, 0.0)).astype(
        jnp.bfloat16
    )


def body(operator, recorded, filter_coefficients, tap_delays):
    local_rows = operator.shape[1]
    gather_total = recorded.shape[3]
    own_block = operator[0]
    segment = lax.all_gather(recorded, "row", axis=1, tiled=True)
    signal_length = segment.shape[1]
    columns = own_block.reshape(local_rows, 2 * signal_length)
    product = complex_block(columns, segment[0])
    spectra = product.astype(jnp.bfloat16).reshape(1, local_rows, 2, gather_total)
    predicted_traces, recorded_traces = (
        lax.all_to_all(spectra, "freq", split_axis=1, concat_axis=0, tiled=True),
        lax.all_to_all(recorded, "freq", split_axis=1, concat_axis=0, tiled=True),
    )
    table = inverse_lookup(predicted_traces.shape[0], NT)

    def to_time(traces):
        return jnp.einsum(
            "frcs,fct->rst", traces, table, preferred_element_type=jnp.float32
        ).astype(jnp.bfloat16)

    data_time = to_time(recorded_traces)
    border_rows = to_time(padded_2(predicted_traces, (("freq", 1),), 1))
    estimate = match_filter(
        border_rows, filter_coefficients, tap_delays, predicted_traces.shape[1], NT
    )
    return shrink(data_time, estimate)


def solution(mesh):
    in_specs = (
        P("freq", "row", None, None),
        P("freq", "row", None, None),
        P(None, None, ("row", "freq")),
        P(),
    )
    out_specs = P(("row", "freq"), None, None)
    return jax.shard_map(body, mesh=mesh, in_specs=in_specs, out_specs=out_specs, check_vma=False)
```

profile of v0, /device:TPU:11, one launch (start us, length us, event | category | flops | bytes accessed | tf_op | source)
XLA Modules:
  0.0 656.7 jit_solution(17252754905582921250)
XLA Ops:
  6.5 0.0 copy-start
  6.5 0.0 all-gather.2.cloned.1.call-start
  6.5 1.9 copy.20
  8.4 0.0 all-gather.2.cloned.1.call-update
  8.5 1.5 copy.33
  10.0 23.1 %all-gather.2.cloned.1.call-done = bf16[1,1024,2,512]{3,1,2,0:T(8,128)(2,1)} async-done(((bf16[1,256,2,512]{3,1,2,0:T(8,128)(2,1)}), bf16[1,1024,2,512]{3,1,2,0:T(8,128)(2,1)}) %all-gather.2.cloned.1.call-update) | async-done | bytes 2097168 | tf_op jit(solution)/shard_map/all_gather | solution.py:78
  33.1 1.3 fusion.26
  34.4 1.7 slice_bitcast_fusion
  36.1 1.3 fusion.8
  37.4 1.2 copy.21
  38.5 5.5 all-to-all-start.1
  44.0 0.8 slice_bitcast_fusion.24
  44.8 1.0 slice_bitcast_fusion.25
  45.8 0.2 multiply_convert_fusion.2
  46.0 10.0 %all-to-all-done.1 = bf16[1,256,2,512]{3,2,0,1:T(2,128)(2,1)S(1)} async-done(((bf16[1,256,2,512]{3,2,0,1:T(2,128)(2,1)}), bf16[1,256,2,512]{3,2,0,1:T(2,128)(2,1)S(1)}, u32[]{:S(2)}, u32[]{:S(2)}) %all-to-all-start.1) | async-done | bytes 524320 | tf_op jit(solution)/shard_map/all_to_all | solution.py:84
  56.0 6.3 all-to-all-start
  62.3 0.1 copy.22
  62.4 0.3 copy.23
  62.7 3.1 collective-permute-start
  65.8 2.2 collective-permute-start.1
  68.0 0.0 copy-done
  68.0 0.7 fusion.28
  78.6 0.0 collective-permute-done
  78.6 0.0 collective-permute-done.1
  78.6 14.9 %bitcast_convert_fusion = bf16[34,512,1024]{1,2,0:T(8,128)(2,1)} fusion(bf16[8,1,2,512]{3,0,2,1:T(8,128)(2,1)S(1)} %collective-permute-done.1, bf16[8,32,2,512]{3,0,2,1:T(8,128)(2,1)S(1)} %copy.23, bf16[8,1,2,512]{3,0,2,1:T(8,128)(2,1)S(1)} %collective-permute-done, bf16[8,1,1024]{2,0,1:T(8,128)(2,1)S(1)} %get-tuple-element.34, ...), kind=kOutput, calls=%fused_computation | convolution fusion | flops 588824576 | bytes 36241408 | tf_op jit(solution)/shard_map/frcs,fct->rst/dot_general | solution.py:90
  93.5 0.0 all-to-all-done
  93.5 512.2 %multiply_convert_fusion = bf16[32,512,1024]{1,2,0:T(8,128)(2,1)} fusion(s32[]{:T(128)S(6)} %add.190, s32[]{:T(128)S(6)} %select_n.52, s32[]{:T(128)S(6)} %add.189, s32[]{:T(128)S(6)} %select_n.51, s32[]{:T(128)S(6)} %select_n.50, s32[]{:T(128)S(6)} %select_n.49, s32[]{:T(128)S(6)} %select_n.48, s32[]{:T(128)S(6)} %select_n.47, s32[]{:T(128)S(6)} %select_n.46, ...), kind=kOutput, calls=%fused_computation.3 | convolution fusion | flops 1879113728 | bytes 69766184 | tf_op jit(solution)/shard_map/frcs,fct->rst/dot_general | solution.py:90
  605.7 44.2 %copy.27 = bf16[32,512,1024]{2,1,0:T(8,128)(2,1)} copy(bf16[32,512,1024]{1,2,0:T(8,128)(2,1)} %multiply_convert_fusion) | data formatting | bytes 67108864 | tf_op jit(solution)/shard_map/convert_element_type | solution.py:69
  (2 shorter events, 0.0 us)
Async XLA Ops:
  6.5 61.5 %copy-start = (s32[8]{0:T(128)S(1)}, s32[8]{0:T(128)}, u32[]{:S(2)}) copy-start(s32[8]{0:T(128)} %param.7) | copy-start | bytes 100
  6.5 26.5 %all-gather.2.cloned.1.call-start = ((), (), s32[]{:S(2)}) async-start(), calls=%async_computation.2 | async-start | bytes 2621440 | tf_op jit(solution)/shard_map/all_gather | solution.py:78
  38.5 17.4 %all-to-all-start.1 = ((bf16[1,256,2,512]{3,2,0,1:T(2,128)(2,1)}), bf16[1,256,2,512]{3,2,0,1:T(2,128)(2,1)S(1)}, u32[]{:S(2)}, u32[]{:S(2)}) async-start(bf16[1,256,2,512]{3,2,0,1:T(2,128)(2,1)} %copy.21), calls=%async_computation.1 | async-start | bytes 1048576 | tf_op jit(solution)/shard_map/all_to_all | solution.py:84
  56.0 37.5 %all-to-all-start = ((bf16[1,256,2,512]{3,2,0,1:T(2,128)(2,1)}), bf16[1,256,2,512]{3,2,0,1:T(2,128)(2,1)S(1)}, u32[]{:S(2)}, u32[]{:S(2)}) async-start(bf16[1,256,2,512]{3,2,0,1:T(2,128)(2,1)} %bitcast.102), calls=%async_computation | async-start | bytes 1048576 | tf_op jit(solution)/shard_map/all_to_all | solution.py:85
  62.7 15.9 %collective-permute-start = (bf16[8,1,2,512]{3,0,2,1:T(8,128)(2,1)S(1)}, bf16[8,1,2,512]{3,0,2,1:T(8,128)(2,1)S(1)}, u32[]{:S(2)}, u32[]{:S(2)}) collective-permute-start(bf16[8,1,2,512]{3,0,2,1:T(8,128)(2,1)S(1)} %get-tuple-element.7), channel_id=1, source_target_pairs={{0,4},{4,8},{8,12},{12,16},{16,20},{20,24},{24,28},{1,5},{5,9},{9,... | collective-permute-start | bytes 49160 | tf_op jit(solution)/shard_map/ppermute | solution.py:20
  65.8 12.8 %collective-permute-start.1 = (bf16[8,1,2,512]{3,0,2,1:T(8,128)(2,1)S(1)}, bf16[8,1,2,512]{3,0,2,1:T(8,128)(2,1)S(1)}, u32[]{:S(2)}, u32[]{:S(2)}) collective-permute-start(bf16[8,1,2,512]{3,0,2,1:T(8,128)(2,1)S(1)} %get-tuple-element.8), channel_id=1, source_target_pairs={{4,0},{8,4},{12,8},{16,12},{20,16},{24,20},{28,24},{5,1},{9,5},{13... | collective-permute-start | bytes 49160 | tf_op jit(solution)/shard_map/ppermute | solution.py:23
Sparse Core Ops, SparseCore 0:
  8.9 24.1 all-gather.1
where the time goes:
time: 660 us; the launch traced here: 657 us
  matrix products  528 us (80%)
  local copies, waits for them, and re-layouts  53.2 us (8%)
  waiting for transfers between devices  33.1 us (5%)
  between operations  23.4 us (4%)
  starting transfers between devices  17.1 us (3%)
    dot_general x2, matrix products, to_time(): jnp.einsum('frcs,fct->rst', traces, table, preferred_element_type=jnp.flo...  527 us
    convert_element_type x1, local copies, waits for them, and re-layouts, shrink(): (jnp.sign(residual) * jnp.maximum(jnp.abs(residual) - shrink_level, 0.0))...  44.2 us
    all_gather x1, waiting for transfers between devices, body(): segment = lax.all_gather(recorded, 'row', axis=1, tiled=True)  23.1 us
  transfers between devices with their start and end apart: 5, of which 2 were waited for; matrix products, arithmetic and copies ran while one was open for 3% of the time, Pallas kernels for 0%

commit v1 on v0

v1 whole, which is shorter than its diff:
```python
import functools
import math

import jax
import jax.numpy as jnp
from jax import lax
from jax.experimental import pallas as pl
from jax.experimental.pallas import tpu as pltpu
from jax.sharding import PartitionSpec as P

NT = 1024

shrink_level = 0.5


def inverse_lookup(harmonics, time_step_total):
    overtone_indices = jnp.arange(harmonics) + 1
    recording_epochs = jnp.arange(time_step_total)
    rotation_radians = (
        overtone_indices[:, None] * recording_epochs[None, :] % time_step_total
    ).astype(jnp.float32) * (2.0 * math.pi / time_step_total)
    scale = 1.0 / math.sqrt(harmonics)
    return jnp.stack(
        [jnp.cos(rotation_radians) * scale, -jnp.sin(rotation_radians) * scale], axis=1
    ).astype(jnp.bfloat16)


def time_kernel(
    per_step, weights_ref, delays_ref, table_ref, recorded_ref, predicted_ref, out_ref, shifted, basis
):
    taps, depth, times = shifted.shape
    step = pl.program_id(0)
    part = min(depth, 16)

    @pl.when(step == 0)
    def _():
        @pl.loop(0, depth // part)
        def _(block):
            at = pl.ds(pl.multiple_of(block * part, part), part)
            table = table_ref[at, :].astype(jnp.float32)
            position = lax.broadcasted_iota(jnp.int32, table.shape, 1)
            for tap in range(taps):
                delay = delays_ref[tap]
                moved = pltpu.roll(table, delay, 1)
                shifted[tap, at, :] = jnp.where(position >= delay, moved, 0.0)
            for slot in range(per_step):
                basis[slot, at, :] = table_ref[at, :]

    for slot in range(per_step):
        station = step * per_step + slot

        @pl.loop(0, depth // part)
        def _(block):
            at = pl.multiple_of(block * part, part)
            for column in range(0, times, 512):
                columns = pl.ds(column, 512)
                moved = [shifted[tap, pl.ds(at, part), columns] for tap in range(taps)]
                for neighbour in range(3):
                    total = moved[0] * -weights_ref[neighbour, 0, station]
                    for tap in range(1, taps):
                        total = total - moved[tap] * weights_ref[neighbour, tap, station]
                    rows = pl.ds(pl.multiple_of((neighbour + 1) * depth + at, part), part)
                    basis[slot, rows, columns] = total.astype(jnp.bfloat16)

        spectra = jnp.concatenate(
            [recorded_ref[station]] + [predicted_ref[station + n] for n in range(3)], axis=0
        )
        for column in range(0, times, 256):
            residual = lax.dot_general(
                spectra,
                basis[slot, :, column : column + 256],
                (((0,), (0,)), ((), ())),
                preferred_element_type=jnp.float32,
            )
            clipped = jnp.clip(residual, -shrink_level, shrink_level)
            out_ref[slot, :, column : column + 256] = (residual - clipped).astype(jnp.bfloat16)


def to_primaries(weights, delays, table, recorded, predicted):
    rows, depth, columns = recorded.shape
    taps, times = weights.shape[1], table.shape[1]
    per_step = 2 if rows % 2 == 0 else 1
    return pl.pallas_call(
        functools.partial(time_kernel, per_step),
        grid=(rows // per_step,),
        out_shape=jax.ShapeDtypeStruct((rows, columns, times), jnp.bfloat16),
        in_specs=[
            pl.BlockSpec(memory_space=pltpu.SMEM),
            pl.BlockSpec(memory_space=pltpu.SMEM),
            pl.BlockSpec(memory_space=pltpu.VMEM),
            pl.BlockSpec(memory_space=pltpu.VMEM),
            pl.BlockSpec(memory_space=pltpu.VMEM),
        ],
        out_specs=pl.BlockSpec((per_step, columns, times), lambda i: (i, 0, 0)),
        scratch_shapes=[
            pltpu.VMEM((taps, depth, times), jnp.float32),
            pltpu.VMEM((per_step, 4 * depth, times), jnp.bfloat16),
        ],
        compiler_params=pltpu.CompilerParams(vmem_limit_bytes=40 * 1024 * 1024),
        cost_estimate=pl.CostEstimate(
            flops=8 * rows * columns * depth * times,
            bytes_accessed=2 * rows * columns * times,
            transcendentals=0,
        ),
    )(weights, delays, table, recorded, predicted)


def body(operator, recorded, filter_coefficients, tap_delays):
    stations = operator.shape[1]
    tiles = lax.axis_size("freq")
    rows = stations // tiles
    shots = recorded.shape[3]
    recorded_tiles = lax.all_to_all(
        recorded[0].reshape(tiles, rows, 2, shots), "freq", split_axis=0, concat_axis=0, tiled=True
    )
    segment = lax.all_gather(recorded[0], "row", axis=0, tiled=True)
    segment = segment.reshape(segment.shape[0], 2 * shots)
    with_real = jnp.dot(operator[0, :, 0], segment, preferred_element_type=jnp.float32)
    with_imag = jnp.dot(operator[0, :, 1], segment, preferred_element_type=jnp.float32)
    predicted = jnp.stack(
        [
            with_real[:, :shots] - with_imag[:, shots:],
            with_real[:, shots:] + with_imag[:, :shots],
        ],
        axis=1,
    ).astype(jnp.bfloat16)
    inner = predicted.reshape(tiles, rows, 2, shots)
    nothing = jnp.zeros((1, 1, 2, shots), jnp.bfloat16)
    before = jnp.concatenate([nothing, inner[:-1, -1:]], axis=0)
    after = jnp.concatenate([inner[1:, :1], nothing], axis=0)
    predicted_tiles = lax.all_to_all(
        jnp.concatenate([before, inner, after], axis=1),
        "freq",
        split_axis=0,
        concat_axis=0,
        tiled=True,
    )
    table = inverse_lookup(tiles, NT).reshape(2 * tiles, NT)

    def by_station(spectra):
        return jnp.swapaxes(spectra, 0, 1).reshape(spectra.shape[1], 2 * tiles, shots)

    return to_primaries(
        filter_coefficients,
        tap_delays,
        table,
        by_station(recorded_tiles),
        by_station(predicted_tiles),
    )


def solution(mesh):
    in_specs = (
        P("freq", "row", None, None),
        P("freq", "row", None, None),
        P(None, None, ("row", "freq")),
        P(),
    )
    out_specs = P(("row", "freq"), None, None)
    return jax.shard_map(body, mesh=mesh, in_specs=in_specs, out_specs=out_specs, check_vma=False)
```

time: 660 us -> 88.6 us (0.13)
  the two profiles are of different devices: /device:TPU:11 before, /device:TPU:0 now
where the time goes in v1:
time: 88.6 us; the launch traced here: 88.3 us
  waiting for transfers between devices  32.4 us (37%)
  Pallas kernels  18.4 us (21%)
  between operations  13.5 us (15%)
  starting transfers between devices  12.8 us (14%)
  local copies, waits for them, and re-layouts  7.18 us (8%)
  other arithmetic  2.52 us (3%)
  matrix products  1.45 us (2%)
    pallas_call x1, Pallas kernels, to_primaries(): pl.pallas_call(functools.partial(time_kernel, per_step), grid=(rows // pe...  18.4 us
    all_gather x1, waiting for transfers between devices, body(): segment = lax.all_gather(recorded[0], 'row', axis=0, tiled=True)  18.2 us
    all_to_all x1, waiting for transfers between devices, body(): lax.all_to_all(jnp.concatenate([before, inner, after], axis=1), 'freq', s...  13.5 us
    all_to_all x1, starting transfers between devices, body(): lax.all_to_all(recorded[0].reshape(tiles, rows, 2, shots), 'freq', split_...  7.26 us
    all_to_all x1, starting transfers between devices, body(): lax.all_to_all(jnp.concatenate([before, inner, after], axis=1), 'freq', s...  5.51 us
    unnamed x7, local copies, waits for them, and re-layouts  2.17 us
    transpose x2, local copies, waits for them, and re-layouts, by_station(): jnp.swapaxes(spectra, 0, 1).reshape(spectra.shape[1], 2 * tiles, shots)  2.17 us
    concatenate x1, other arithmetic, body(): jnp.concatenate([before, inner, after], axis=1)  1.96 us
  transfers between devices with their start and end apart: 3, of which 2 were waited for; matrix products, arithmetic and copies ran while one was open for 12% of the time, Pallas kernels for 0%

profile of v1, /device:TPU:0, one launch (start us, length us, event | category | flops | bytes accessed | tf_op | source)
XLA Modules:
  0.0 88.3 jit_solution(11340456224174275580)
XLA Ops:
  6.5 0.0 copy-start.2
  6.5 0.0 all-gather.3.cloned.1.call-start
  6.5 0.7 all-gather.3.cloned.1.call-update
  7.3 7.3 %all-to-all-start = ((bf16[8,32,2,512]{3,2,1,0:T(2,128)(2,1)}), bf16[8,32,2,512]{3,2,1,0:T(2,128)(2,1)}, u32[]{:S(2)}, u32[]{:S(2)}) async-start(bf16[8,32,2,512]{3,2,1,0:T(2,128)(2,1)} %bitcast.23), calls=%async_computation | async-start | bytes 1048576 | tf_op jit(solution)/shard_map/all_to_all | solution.py:113
  14.5 0.0 copy-done.2
  14.5 1.5 %fusion.16 = (bf16[1,256,1,1024]{3,2,1,0:T(2,128)(2,1)S(1)}, bf16[1,256,1,1024]{3,2,1,0:T(2,128)(2,1)S(1)}) fusion(bf16[1,256,2,1024]{3,2,1,0:T(2,128)(2,1)S(1)} %copy-done.2), kind=kLoop, calls=%fused_computation.30 | loop fusion | bytes 2097152 | tf_op jit(solution)/shard_map/slice | solution.py:118
  16.0 18.2 %all-gather.3.cloned.1.call-done = bf16[1,1024,2,512]{3,2,0,1:T(2,128)(2,1)} async-done(((bf16[1,256,2,512]{3,2,0,1:T(2,128)(2,1)}), bf16[1,1024,2,512]{3,2,0,1:T(2,128)(2,1)}) %all-gather.3.cloned.1.call-update) | async-done | bytes 2097168 | tf_op jit(solution)/shard_map/all_gather | solution.py:116
  34.2 2.2 %copy.30 = bf16[128,8,2,512]{3,1,2,0:T(8,128)(2,1)S(1)} copy(bf16[128,8,2,512]{3,2,1,0:T(2,128)(2,1)} %bitcast.21) | data formatting | bytes 4194304
  36.4 0.7 fusion.3
  37.1 0.7 fusion.2
  37.9 0.3 fusion.1
  38.1 0.4 copy.26
  38.6 0.4 copy.25
  39.0 0.1 fusion.14
  39.1 2.0 %pad_maximum_fusion = bf16[8,34,2,512]{3,2,1,0:T(2,128)(2,1)} fusion(bf16[8,1,2,512]{3,2,1,0:T(2,128)(2,1)S(1)} %get-tuple-element.8, bf16[8,32,1,512]{3,2,1,0:T(2,128)(2,1)S(1)} %copy.26, bf16[8,32,1,512]{3,2,1,0:T(2,128)(2,1)S(1)} %copy.25, bf16[8,1,2,512]{3,2,1,0:T(2,128)(2,1)S(1)} %get-tuple-element.7), kind=kLoop, calls=%fused_computation | loop fusion | flops 2228224 | bytes 1114112 | tf_op jit(solution)/shard_map/concatenate | solution.py:132
  41.1 0.0 all-to-all-done
  41.1 5.5 %all-to-all-start.1 = ((bf16[8,34,2,512]{3,2,1,0:T(2,128)(2,1)}), bf16[8,34,2,512]{3,2,1,0:T(2,128)(2,1)S(1)}, u32[]{:S(2)}, u32[]{:S(2)}) async-start(bf16[8,34,2,512]{3,2,1,0:T(2,128)(2,1)} %pad_maximum_fusion), calls=%async_computation.1 | async-start | bytes 1114112 | tf_op jit(solution)/shard_map/all_to_all | solution.py:131
  46.6 0.2 multiply_convert_fusion.1
  46.9 0.0 copy-start
  46.9 0.0 copy-start.1
  46.9 1.6 %copy.21 = bf16[32,8,2,512]{3,2,1,0:T(2,128)(2,1)S(1)} copy(bf16[32,8,2,512]{3,2,0,1:T(2,128)(2,1)} %bitcast.1) | data formatting | bytes 1048576 | tf_op jit(solution)/shard_map/transpose | solution.py:141
  48.5 0.2 reshape.125.recorded_ref
  48.7 13.5 %all-to-all-done.1 = bf16[8,34,2,512]{3,2,1,0:T(2,128)(2,1)S(1)} async-done(((bf16[8,34,2,512]{3,2,1,0:T(2,128)(2,1)}), bf16[8,34,2,512]{3,2,1,0:T(2,128)(2,1)S(1)}, u32[]{:S(2)}, u32[]{:S(2)}) %all-to-all-start.1) | async-done | bytes 557088 | tf_op jit(solution)/shard_map/all_to_all | solution.py:131
  62.2 0.6 copy.27
  62.8 0.2 reshape.127.predicted_ref
  63.0 0.0 copy-done
  63.0 0.0 copy-done.1
  63.0 18.4 %shard_map.46 = bf16[32,512,1024]{2,1,0:T(8,128)(2,1)} custom-call(f32[3,8,32]{2,1,0:T(8,128)S(1)} %copy-done, s32[8]{0:T(128)S(1)} %copy-done.1, bf16[16,1024]{1,0:T(8,128)(2,1)S(1)} %convert_element_type.24.table_ref, bf16[32,16,512]{2,1,0:T(8,128)(2,1)S(1)} %reshape.125.recorded_ref, bf16[34,16,512]{2,1,0:T(8,128)(2,1)S(1)} %reshape.127.predicted_ref), custom_call_target="tpu_custom_call" | custom-call | flops 2147483648 | bytes 33554432 | tf_op jit(solution)/shard_map/pallas_call | solution.py:83
  (4 shorter events, 0.1 us)
Async XLA Ops:
  6.5 8.0 %copy-start.2 = (bf16[1,256,2,1024]{3,2,1,0:T(2,128)(2,1)S(1)}, bf16[1,256,2,1024]{3,2,1,0:T(2,128)(2,1)}, u32[]{:S(2)}) copy-start(bf16[1,256,2,1024]{3,2,1,0:T(2,128)(2,1)} %param.4) | copy-start | bytes 3145732
  6.5 27.7 %all-gather.3.cloned.1.call-start = ((), (), s32[]{:S(2)}) async-start(), calls=%async_computation.2 | async-start | bytes 2621440 | tf_op jit(solution)/shard_map/all_gather | solution.py:116
  7.3 33.8 %all-to-all-start = ((bf16[8,32,2,512]{3,2,1,0:T(2,128)(2,1)}), bf16[8,32,2,512]{3,2,1,0:T(2,128)(2,1)}, u32[]{:S(2)}, u32[]{:S(2)}) async-start(bf16[8,32,2,512]{3,2,1,0:T(2,128)(2,1)} %bitcast.23), calls=%async_computation | async-start | bytes 1048576 | tf_op jit(solution)/shard_map/all_to_all | solution.py:113
  41.1 21.1 %all-to-all-start.1 = ((bf16[8,34,2,512]{3,2,1,0:T(2,128)(2,1)}), bf16[8,34,2,512]{3,2,1,0:T(2,128)(2,1)S(1)}, u32[]{:S(2)}, u32[]{:S(2)}) async-start(bf16[8,34,2,512]{3,2,1,0:T(2,128)(2,1)} %pad_maximum_fusion), calls=%async_computation.1 | async-start | bytes 1114112 | tf_op jit(solution)/shard_map/all_to_all | solution.py:131
  46.9 16.1 %copy-start = (f32[3,8,32]{2,1,0:T(8,128)S(1)}, f32[3,8,32]{2,1,0:T(8,128)}, u32[]{:S(2)}) copy-start(f32[3,8,32]{2,1,0:T(8,128)} %weights_ref.1) | copy-start | bytes 9220
  46.9 16.1 %copy-start.1 = (s32[8]{0:T(128)S(1)}, s32[8]{0:T(128)}, u32[]{:S(2)}) copy-start(s32[8]{0:T(128)} %delays_ref.1) | copy-start | bytes 100
Sparse Core Ops, SparseCore 0:
  8.9 25.2 all-gather.2

commit v2 on v1

--- a/solution.py
+++ b/solution.py
@@ -9,6 +9,7 @@
 from jax.sharding import PartitionSpec as P
 
 NT = 1024
+MESH = pl.DeviceIdType.MESH
 
 shrink_level = 0.5
 
@@ -105,36 +106,218 @@
     )(weights, delays, table, recorded, predicted)
 
 
+def exchange_kernel(
+    tiles,
+    lines,
+    real_ref,
+    imag_ref,
+    shard_ref,
+    recorded_ref,
+    recorded_out,
+    predicted_out,
+    halo_out,
+    segment,
+    product,
+    predicted,
+    halo,
+    recorded_sent,
+    recorded_got,
+    predicted_sent,
+    predicted_got,
+    halo_sent,
+    halo_got,
+    own_sent,
+    forward_sent,
+    shard_got,
+):
+    mine = lax.axis_index("freq")
+    line = lax.axis_index("row")
+    sibling = line + 1 - 2 * (line % 2)
+    peers = [(line + 2 * k) % lines for k in range(1, lines // 2)]
+    stations, width = shard_ref.shape
+    shots = width // 2
+    rows = stations // tiles
+
+    barrier = pltpu.get_barrier_semaphore()
+
+    @pl.loop(1, tiles)
+    def _(k):
+        pl.semaphore_signal(
+            barrier, inc=1, device_id={"freq": (mine + k) % tiles}, device_id_type=MESH
+        )
+
+    for peer in [sibling] + peers:
+        pl.semaphore_signal(barrier, inc=1, device_id={"row": peer}, device_id_type=MESH)
+    pl.semaphore_wait(barrier, tiles - 1 + 1 + len(peers))
+
+    def own_copy(slot, peer):
+        return pltpu.make_async_remote_copy(
+            src_ref=shard_ref,
+            dst_ref=segment.at[line],
+            send_sem=own_sent.at[slot],
+            recv_sem=shard_got.at[line],
+            device_id={"row": peer},
+            device_id_type=MESH,
+        )
+
+    def forward_copy(slot, source):
+        return pltpu.make_async_remote_copy(
+            src_ref=segment.at[source],
+            dst_ref=segment.at[source],
+            send_sem=forward_sent.at[slot],
+            recv_sem=shard_got.at[source],
+            device_id={"row": sibling},
+            device_id_type=MESH,
+        )
+
+    def tile_copy(source, target, sent, got, tile):
+        return pltpu.make_async_remote_copy(
+            src_ref=source.at[tile],
+            dst_ref=target.at[mine],
+            send_sem=sent.at[tile],
+            recv_sem=got.at[mine],
+            device_id={"freq": tile},
+            device_id_type=MESH,
+        )
+
+    def tile_arrival(source, target, sent, got, tile):
+        return pltpu.make_async_remote_copy(
+            src_ref=source.at[tile],
+            dst_ref=target.at[tile],
+            send_sem=sent.at[tile],
+            recv_sem=got.at[tile],
+            device_id={"freq": tile},
+            device_id_type=MESH,
+        )
+
+    for slot, peer in enumerate(peers):
+        own_copy(slot, peer).start()
+    own_copy(len(peers), sibling).start()
+
+    recorded_set = (recorded_ref, recorded_out, recorded_sent, recorded_got)
+    predicted_set = (predicted, predicted_out, predicted_sent, predicted_got)
+    halo_set = (halo, halo_out, halo_sent, halo_got)
+
+    @pl.loop(1, tiles)
+    def _(k):
+        tile_copy(*recorded_set, (mine + k) % tiles).start()
+
+    recorded_out[mine] = recorded_ref[mine]
+
+    def accumulate(source, block, first):
+        at = pl.ds(pl.multiple_of(source * stations, stations), stations)
+        with_real = jnp.dot(real_ref[:, at], block[...], preferred_element_type=jnp.float32)
+        with_imag = jnp.dot(imag_ref[:, at], block[...], preferred_element_type=jnp.float32)
+        upper = with_real[:, :shots] - with_imag[:, shots:]
+        lower = with_real[:, shots:] + with_imag[:, :shots]
+        if not first:
+            upper = upper + product[:, :shots]
+            lower = lower + product[:, shots:]
+        product[:, :shots] = upper
+        product[:, shots:] = lower
+
+    accumulate(line, shard_ref, True)
+    forward_copy(0, sibling).wait_recv()
+    accumulate(sibling, segment.at[sibling], False)
+    for slot, peer in enumerate(peers):
+        forward_copy(slot, peer).wait_recv()
+        forward_copy(slot, peer).start()
+        accumulate(peer, segment.at[peer], False)
+    for slot, peer in enumerate(peers):
+        other = peer + 1 - 2 * (peer % 2)
+        forward_copy(slot, other).wait_recv()
+        accumulate(other, segment.at[other], False)
+
+    @pl.loop(1, tiles + 1)
+    def _(k):
+        tile = (mine + k) % tiles
+        if rows % 16 == 0:
+            start = pl.multiple_of(tile * rows, 16)
+            inner = product[pl.ds(start, rows), :]
+        else:
+            inner = jnp.concatenate(
+                [product[pl.ds(tile * rows + i, 1), :] for i in range(rows)], axis=0
+            )
+        predicted[tile] = inner.astype(jnp.bfloat16)
+        low = product[pl.ds(jnp.maximum(tile * rows - 1, 0), 1), :]
+        high = product[pl.ds(jnp.minimum(tile * rows + rows, stations - 1), 1), :]
+        low = jnp.where(tile == 0, 0.0, low)
+        high = jnp.where(tile == tiles - 1, 0.0, high)
+        pieces = [edge[:, i : i + 128] for edge in (low, high) for i in range(0, width, 128)]
+        halo[tile] = jnp.concatenate(pieces, axis=0).astype(jnp.bfloat16)
+
+        @pl.when(k < tiles)
+        def _():
+            tile_copy(*predicted_set, tile).start()
+            tile_copy(*halo_set, tile).start()
+
+    predicted_out[mine] = predicted[mine]
+    halo_out[mine] = halo[mine]
+
+    @pl.loop(1, tiles)
+    def _(k):
+        for transfers in (recorded_set, predicted_set, halo_set):
+            tile_arrival(*transfers, (mine + k) % tiles).wait_recv()
+
+    @pl.loop(1, tiles)
+    def _(k):
+        for transfers in (recorded_set, predicted_set, halo_set):
+            tile_copy(*transfers, (mine + k) % tiles).wait_send()
+
+    for slot, peer in enumerate(peers):
+        own_copy(slot, peer).wait_send()
+        forward_copy(slot, peer).wait_send()
+    own_copy(len(peers), sibling).wait_send()
+
+
+def exchange(real, imag, shard, tiles, lines):
+    stations, width = shard.shape
+    rows = stations // tiles
+    vmem = pl.BlockSpec(memory_space=pltpu.VMEM)
+    tile_shape = (tiles, rows, width)
+    halo_shape = (tiles, 2 * width // 128, 128)
+    sems = pltpu.SemaphoreType.DMA((tiles,))
+    return pl.pallas_call(
+        functools.partial(exchange_kernel, tiles, lines),
+        out_shape=[
+            jax.ShapeDtypeStruct(tile_shape, jnp.bfloat16),
+            jax.ShapeDtypeStruct(tile_shape, jnp.bfloat16),
+            jax.ShapeDtypeStruct(halo_shape, jnp.bfloat16),
+        ],
+        in_specs=[vmem] * 4,
+        out_specs=[vmem] * 3,
+        scratch_shapes=[
+            pltpu.VMEM((lines, stations, width), jnp.bfloat16),
+            pltpu.VMEM((stations, width), jnp.float32),
+            pltpu.VMEM(tile_shape, jnp.bfloat16),
+            pltpu.VMEM(halo_shape, jnp.bfloat16),
+        ]
+        + [sems] * 6
+        + [pltpu.SemaphoreType.DMA((lines,))] * 3,
+        compiler_params=pltpu.CompilerParams(
+            collective_id=0, has_side_effects=True, vmem_limit_bytes=40 * 1024 * 1024
+        ),
+        cost_estimate=pl.CostEstimate(
+            flops=8 * lines * stations * stations * width // 2,
+            bytes_accessed=2 * (lines + 5) * stations * width,
+            transcendentals=0,
+        ),
+    )(real, imag, shard, shard.reshape(tile_shape))
+
+
 def body(operator, recorded, filter_coefficients, tap_delays):
     stations = operator.shape[1]
-    tiles = lax.axis_size("freq")
+    tiles, lines = lax.axis_size("freq"), lax.axis_size("row")
     rows = stations // tiles
     shots = recorded.shape[3]
-    recorded_tiles = lax.all_to_all(
-        recorded[0].reshape(tiles, rows, 2, shots), "freq", split_axis=0, concat_axis=0, tiled=True
+    recorded_tiles, predicted_tiles, halo = exchange(
+        operator[0, :, 0],
+        operator[0, :, 1],
+        recorded[0].reshape(stations, 2 * shots),
+        tiles,
+        lines,
     )
-    segment = lax.all_gather(recorded[0], "row", axis=0, tiled=True)
-    segment = segment.reshape(segment.shape[0], 2 * shots)
-    with_real = jnp.dot(operator[0, :, 0], segment, preferred_element_type=jnp.float32)
-    with_imag = jnp.dot(operator[0, :, 1], segment, preferred_element_type=jnp.float32)
-    predicted = jnp.stack(
-        [
-            with_real[:, :shots] - with_imag[:, shots:],
-            with_real[:, shots:] + with_imag[:, :shots],
-        ],
-        axis=1,
-    ).astype(jnp.bfloat16)
-    inner = predicted.reshape(tiles, rows, 2, shots)
-    nothing = jnp.zeros((1, 1, 2, shots), jnp.bfloat16)
-    before = jnp.concatenate([nothing, inner[:-1, -1:]], axis=0)
-    after = jnp.concatenate([inner[1:, :1], nothing], axis=0)
-    predicted_tiles = lax.all_to_all(
-        jnp.concatenate([before, inner, after], axis=1),
-        "freq",
-        split_axis=0,
-        concat_axis=0,
-        tiled=True,
-    )
+    halo = halo.reshape(tiles, 2, 2 * shots)
     table = inverse_lookup(tiles, NT).reshape(2 * tiles, NT)
 
     def by_station(spectra):
@@ -145,7 +328,7 @@
         tap_delays,
         table,
         by_station(recorded_tiles),
-        by_station(predicted_tiles),
+        by_station(jnp.concatenate([halo[:, :1], predicted_tiles, halo[:, 1:]], axis=1)),
     )
 
 

time: 88.6 us -> 56.7 us (0.64)
  the two profiles are of different devices: /device:TPU:0 before, /device:TPU:11 now
where the time goes in v2:
time: 56.7 us; the launch traced here: 56.5 us
  Pallas kernels  51.1 us (90%)
  local copies, waits for them, and re-layouts  4.79 us (8%)
    pallas_call x1, Pallas kernels, exchange(): pl.pallas_call(functools.partial(exchange_kernel, tiles, lines), out_shap...  32.7 us
    pallas_call x1, Pallas kernels, to_primaries(): pl.pallas_call(functools.partial(time_kernel, per_step), grid=(rows // pe...  18.4 us
    slice x1, local copies, waits for them, and re-layouts, body(): operator[0, :, 1]  1.5 us
    unnamed x9, local copies, waits for them, and re-layouts  1.46 us

profile of v2, /device:TPU:11, one launch (start us, length us, event | category | flops | bytes accessed | tf_op | source)
XLA Modules:
  0.0 56.5 jit_solution(6043240215121326734)
XLA Ops:
  0.0 0.0 copy-start.3
  0.0 0.0 copy-start.2
  0.0 0.2 multiply_convert_fusion.1
  0.3 1.3 %copy.16 = bf16[32,8,2,512]{3,1,2,0:T(8,128)(2,1)S(1)} copy(bf16[32,8,2,512]{3,2,1,0:T(2,128)(2,1)} %bitcast.12) | data formatting | bytes 1048576
  1.6 0.0 copy-done.3
  1.6 0.4 reshape_reshape_squeeze.3.recorded_ref
  2.0 0.0 copy-done.2
  2.0 1.5 %fusion.6 = (bf16[1,256,1,1024]{3,2,1,0:T(2,128)(2,1)S(1)}, bf16[1,256,1,1024]{3,2,1,0:T(2,128)(2,1)S(1)}) fusion(bf16[1,256,2,1024]{3,2,1,0:T(2,128)(2,1)S(1)} %copy-done.2), kind=kLoop, calls=%fused_computation.16 | loop fusion | bytes 2097152 | tf_op jit(solution)/shard_map/slice | solution.py:315
  3.5 0.4 copy_bitcast_fusion
  3.9 32.7 %shard_map.46 = (bf16[8,32,1024]{2,1,0:T(8,128)(2,1)S(1)}, bf16[8,32,1024]{2,1,0:T(8,128)(2,1)S(1)}, bf16[8,16,128]{2,1,0:T(8,128)(2,1)S(1)}) custom-call(bf16[256,1024]{1,0:T(8,128)(2,1)S(1)} %get-tuple-element.18.real_ref, bf16[256,1024]{1,0:T(8,128)(2,1)S(1)} %get-tuple-element.17.imag_ref, bf16[256,1024]{1,0:T(8,128)(2,1)S(1)} %bitcast.10, ...), custom_call_target="tpu_custom_call" | custom-call | flops 1073741824 | bytes 4718592 | tf_op jit(solution)/shard_map/pallas_call | solution.py:280
  36.6 0.3 copy.12
  36.9 0.2 reshape.118.recorded_ref
  37.1 0.1 fusion.7
  37.1 0.2 maximum_bitcast_fusion
  37.4 0.0 copy-start
  37.4 0.0 copy-start.1
  37.4 0.3 copy.13
  37.7 0.2 reshape.120.predicted_ref
  37.9 0.2 copy-done
  38.1 0.0 copy-done.1
  38.1 18.4 %shard_map.47 = bf16[32,512,1024]{2,1,0:T(8,128)(2,1)} custom-call(f32[3,8,32]{2,1,0:T(8,128)S(1)} %copy-done, s32[8]{0:T(128)S(1)} %copy-done.1, bf16[16,1024]{1,0:T(8,128)(2,1)S(1)} %convert_element_type.22.table_ref, bf16[32,16,512]{2,1,0:T(8,128)(2,1)S(1)} %reshape.118.recorded_ref, bf16[34,16,512]{2,1,0:T(8,128)(2,1)S(1)} %reshape.120.predicted_ref), custom_call_target="tpu_custom_call" | custom-call | flops 2147483648 | bytes 33554432 | tf_op jit(solution)/shard_map/pallas_call | solution.py:84
  (5 shorter events, 0.1 us)
Async XLA Ops:
  0.0 1.6 %copy-start.3 = (bf16[1,256,2,512]{3,2,1,0:T(2,128)(2,1)S(1)}, bf16[1,256,2,512]{3,2,1,0:T(2,128)(2,1)}, u32[]{:S(2)}) copy-start(bf16[1,256,2,512]{3,2,1,0:T(2,128)(2,1)} %param.5) | copy-start | bytes 1572868
  0.0 2.0 %copy-start.2 = (bf16[1,256,2,1024]{3,2,1,0:T(2,128)(2,1)S(1)}, bf16[1,256,2,1024]{3,2,1,0:T(2,128)(2,1)}, u32[]{:S(2)}) copy-start(bf16[1,256,2,1024]{3,2,1,0:T(2,128)(2,1)} %param.4) | copy-start | bytes 3145732
  37.4 0.7 %copy-start = (f32[3,8,32]{2,1,0:T(8,128)S(1)}, f32[3,8,32]{2,1,0:T(8,128)}, u32[]{:S(2)}) copy-start(f32[3,8,32]{2,1,0:T(8,128)} %weights_ref.1) | copy-start | bytes 9220
  37.4 0.7 %copy-start.1 = (s32[8]{0:T(128)S(1)}, s32[8]{0:T(128)}, u32[]{:S(2)}) copy-start(s32[8]{0:T(128)} %delays_ref.1) | copy-start | bytes 100

commit v3 on v2

--- a/solution.py
+++ b/solution.py
@@ -26,89 +26,102 @@
     ).astype(jnp.bfloat16)
 
 
-def time_kernel(
-    per_step, weights_ref, delays_ref, table_ref, recorded_ref, predicted_ref, out_ref, shifted, basis
-):
-    taps, depth, times = shifted.shape
-    step = pl.program_id(0)
+def delay_kernel(delays_ref, table_ref, shifted_ref):
+    taps, depth, times = shifted_ref.shape
     part = min(depth, 16)
 
-    @pl.when(step == 0)
-    def _():
-        @pl.loop(0, depth // part)
-        def _(block):
-            at = pl.ds(pl.multiple_of(block * part, part), part)
-            table = table_ref[at, :].astype(jnp.float32)
-            position = lax.broadcasted_iota(jnp.int32, table.shape, 1)
-            for tap in range(taps):
-                delay = delays_ref[tap]
-                moved = pltpu.roll(table, delay, 1)
-                shifted[tap, at, :] = jnp.where(position >= delay, moved, 0.0)
-            for slot in range(per_step):
-                basis[slot, at, :] = table_ref[at, :]
-
-    for slot in range(per_step):
-        station = step * per_step + slot
-
+    @pl.loop(0, depth // part)
+    def _(block):
+        at = pl.ds(pl.multiple_of(block * part, part), part)
+        table = table_ref[at, :].astype(jnp.float32)
+        position = lax.broadcasted_iota(jnp.int32, table.shape, 1)
+        for tap in range(taps):
+            delay = delays_ref[tap]
+            moved = pltpu.roll(table, delay, 1)
+            shifted_ref[tap, at, :] = jnp.where(position >= delay, moved, 0.0)
+
+
+def delayed_tables(delays, table):
+    vmem = pl.BlockSpec(memory_space=pltpu.VMEM)
+    return pl.pallas_call(
+        delay_kernel,
+        out_shape=jax.ShapeDtypeStruct(delays.shape + table.shape, jnp.float32),
+        in_specs=[pl.BlockSpec(memory_space=pltpu.SMEM), vmem],
+        out_specs=vmem,
+        compiler_params=pltpu.CompilerParams(vmem_limit_bytes=24 * 1024 * 1024),
+    )(delays, table)
+
+
+def filtered_tables(weights_ref, shifted_ref, basis_ref):
+    taps, depth, times = shifted_ref.shape
+    part = min(depth, 16)
+
+    @pl.loop(0, basis_ref.shape[0])
+    def _(station):
         @pl.loop(0, depth // part)
         def _(block):
             at = pl.multiple_of(block * part, part)
             for column in range(0, times, 512):
                 columns = pl.ds(column, 512)
-                moved = [shifted[tap, pl.ds(at, part), columns] for tap in range(taps)]
+                moved = [shifted_ref[tap, pl.ds(at, part), columns] for tap in range(taps)]
                 for neighbour in range(3):
                     total = moved[0] * -weights_ref[neighbour, 0, station]
                     for tap in range(1, taps):
                         total = total - moved[tap] * weights_ref[neighbour, tap, station]
-                    rows = pl.ds(pl.multiple_of((neighbour + 1) * depth + at, part), part)
-                    basis[slot, rows, columns] = total.astype(jnp.bfloat16)
-
+                    rows = pl.ds(pl.multiple_of(neighbour * depth + at, part), part)
+                    basis_ref[station, rows, columns] = total.astype(jnp.bfloat16)
+
+
+def time_kernel(per_step, table_ref, basis_ref, recorded_ref, predicted_ref, out_ref):
+    step = pl.program_id(0)
+    times = table_ref.shape[1]
+    for slot in range(per_step):
+        station = step * per_step + slot
         spectra = jnp.concatenate(
             [recorded_ref[station]] + [predicted_ref[station + n] for n in range(3)], axis=0
         )
         for column in range(0, times, 256):
+            columns = slice(column, column + 256)
             residual = lax.dot_general(
                 spectra,
-                basis[slot, :, column : column + 256],
+                jnp.concatenate([table_ref[:, columns], basis_ref[slot, :, columns]], axis=0),
                 (((0,), (0,)), ((), ())),
                 preferred_element_type=jnp.float32,
             )
             clipped = jnp.clip(residual, -shrink_level, shrink_level)
-            out_ref[slot, :, column : column + 256] = (residual - clipped).astype(jnp.bfloat16)
-
-
-def to_primaries(weights, delays, table, recorded, predicted):
+            out_ref[slot, :, columns] = (residual - clipped).astype(jnp.bfloat16)
+
+
+def to_primaries(table, basis, recorded, predicted):
     rows, depth, columns = recorded.shape
-    taps, times = weights.shape[1], table.shape[1]
+    times = table.shape[1]
     per_step = 2 if rows % 2 == 0 else 1
+    vmem = pl.BlockSpec(memory_space=pltpu.VMEM)
     return pl.pallas_call(
         functools.partial(time_kernel, per_step),
         grid=(rows // per_step,),
         out_shape=jax.ShapeDtypeStruct((rows, columns, times), jnp.bfloat16),
         in_specs=[
-            pl.BlockSpec(memory_space=pltpu.SMEM),
-            pl.BlockSpec(memory_space=pltpu.SMEM),
-            pl.BlockSpec(memory_space=pltpu.VMEM),
-            pl.BlockSpec(memory_space=pltpu.VMEM),
-            pl.BlockSpec(memory_space=pltpu.VMEM),
+            vmem,
+            pl.BlockSpec((per_step, 3 * depth, times), lambda i: (i, 0, 0)),
+            vmem,
+            vmem,
         ],
         out_specs=pl.BlockSpec((per_step, columns, times), lambda i: (i, 0, 0)),
-        scratch_shapes=[
-            pltpu.VMEM((taps, depth, times), jnp.float32),
-            pltpu.VMEM((per_step, 4 * depth, times), jnp.bfloat16),
-        ],
         compiler_params=pltpu.CompilerParams(vmem_limit_bytes=40 * 1024 * 1024),
         cost_estimate=pl.CostEstimate(
             flops=8 * rows * columns * depth * times,
             bytes_accessed=2 * rows * columns * times,
             transcendentals=0,
         ),
-    )(weights, delays, table, recorded, predicted)
+    )(table, basis, recorded, predicted)
 
 
 def exchange_kernel(
     tiles,
     lines,
+    weights_ref,
+    shifted_ref,
     real_ref,
     imag_ref,
     shard_ref,
@@ -116,6 +129,7 @@
     recorded_out,
     predicted_out,
     halo_out,
+    basis_out,
     segment,
     product,
     predicted,
@@ -253,6 +267,7 @@
 
     predicted_out[mine] = predicted[mine]
     halo_out[mine] = halo[mine]
+    filtered_tables(weights_ref, shifted_ref, basis_out)
 
     @pl.loop(1, tiles)
     def _(k):
@@ -270,7 +285,7 @@
     own_copy(len(peers), sibling).wait_send()
 
 
-def exchange(real, imag, shard, tiles, lines):
+def exchange(weights, shifted, real, imag, shard, tiles, lines):
     stations, width = shard.shape
     rows = stations // tiles
     vmem = pl.BlockSpec(memory_space=pltpu.VMEM)
@@ -283,9 +298,10 @@
             jax.ShapeDtypeStruct(tile_shape, jnp.bfloat16),
             jax.ShapeDtypeStruct(tile_shape, jnp.bfloat16),
             jax.ShapeDtypeStruct(halo_shape, jnp.bfloat16),
+            jax.ShapeDtypeStruct((rows, 3 * shifted.shape[1], shifted.shape[2]), jnp.bfloat16),
         ],
-        in_specs=[vmem] * 4,
-        out_specs=[vmem] * 3,
+        in_specs=[pl.BlockSpec(memory_space=pltpu.SMEM)] + [vmem] * 5,
+        out_specs=[vmem] * 4,
         scratch_shapes=[
             pltpu.VMEM((lines, stations, width), jnp.bfloat16),
             pltpu.VMEM((stations, width), jnp.float32),
@@ -302,7 +318,7 @@
             bytes_accessed=2 * (lines + 5) * stations * width,
             transcendentals=0,
         ),
-    )(real, imag, shard, shard.reshape(tile_shape))
+    )(weights, shifted, real, imag, shard, shard.reshape(tile_shape))
 
 
 def body(operator, recorded, filter_coefficients, tap_delays):
@@ -310,7 +326,10 @@
     tiles, lines = lax.axis_size("freq"), lax.axis_size("row")
     rows = stations // tiles
     shots = recorded.shape[3]
-    recorded_tiles, predicted_tiles, halo = exchange(
+    table = inverse_lookup(tiles, NT).reshape(2 * tiles, NT)
+    recorded_tiles, predicted_tiles, halo, basis = exchange(
+        filter_coefficients,
+        delayed_tables(tap_delays, table),
         operator[0, :, 0],
         operator[0, :, 1],
         recorded[0].reshape(stations, 2 * shots),
@@ -318,15 +337,13 @@
         lines,
     )
     halo = halo.reshape(tiles, 2, 2 * shots)
-    table = inverse_lookup(tiles, NT).reshape(2 * tiles, NT)
 
     def by_station(spectra):
         return jnp.swapaxes(spectra, 0, 1).reshape(spectra.shape[1], 2 * tiles, shots)
 
     return to_primaries(
-        filter_coefficients,
-        tap_delays,
         table,
+        basis,
         by_station(recorded_tiles),
         by_station(jnp.concatenate([halo[:, :1], predicted_tiles, halo[:, 1:]], axis=1)),
     )

time: 56.7 us -> 69.9 us (1.23)
  local copies, waits for them, and re-layouts: 4.79 us -> 16.6 us
  other arithmetic: 0.46 us -> 1.5 us
    unnamed x9 -> x23, local copies, waits for them, and re-layouts: 1.46 us -> 7.17 us
    reshape x2, local copies, waits for them, and re-layouts: 0.36 us -> 4.04 us  [by_station(): jnp.swapaxes(spectra, 0, 1).reshape(spectra.shape[1], 2 * tiles, shots)]
    transpose x2, local copies, waits for them, and re-layouts: 0.61 us -> 2.2 us  [by_station(): jnp.swapaxes(spectra, 0, 1).reshape(spectra.shape[1], 2 * tiles, shots)]
    pallas_call x1, Pallas kernels: 18.4 us -> 17.1 us  [to_primaries(): pl.pallas_call(functools.partial(time_kernel, per_step), grid=(rows // pe...]
    transpose x1, other arithmetic: 0.23 us -> 1.27 us  [by_station(): jnp.swapaxes(spectra, 0, 1).reshape(spectra.shape[1], 2 * tiles, shots)]
    another operation x1, local copies, waits for them, and re-layouts: 0.37 us -> 1.16 us  [exchange(): shard.reshape(tile_shape)]
    pallas_call x1, Pallas kernels: 32.7 us -> 33.4 us  [exchange(): pl.pallas_call(functools.partial(exchange_kernel, tiles, lines), out_shap...]
    pallas_call x0 -> x1, Pallas kernels: none -> 0.73 us  [delayed_tables(): pl.pallas_call(delay_kernel, out_shape=jax.ShapeDtypeStruct(delays.shape...]
where the time goes in v3:
time: 69.9 us; the launch traced here: 69.5 us
  Pallas kernels  51.3 us (73%)
  local copies, waits for them, and re-layouts  16.6 us (24%)
  other arithmetic  1.5 us (2%)
    pallas_call x1, Pallas kernels, exchange(): pl.pallas_call(functools.partial(exchange_kernel, tiles, lines), out_shap...  33.4 us
    pallas_call x1, Pallas kernels, to_primaries(): pl.pallas_call(functools.partial(time_kernel, per_step), grid=(rows // pe...  17.1 us
    unnamed x23, local copies, waits for them, and re-layouts  7.17 us
    reshape x2, local copies, waits for them, and re-layouts, by_station(): jnp.swapaxes(spectra, 0, 1).reshape(spectra.shape[1], 2 * tiles, shots)  4.04 us
    transpose x2, local copies, waits for them, and re-layouts, by_station(): jnp.swapaxes(spectra, 0, 1).reshape(spectra.shape[1], 2 * tiles, shots)  2.2 us
    slice x1, local copies, waits for them, and re-layouts, body(): operator[0, :, 1]  1.48 us

profile of v3, /device:TPU:11, one launch (start us, length us, event | category | flops | bytes accessed | tf_op | source)
XLA Modules:
  0.0 69.5 jit_solution(17157784737279439836)
XLA Ops:
  0.0 0.2 multiply_convert_fusion.1
  0.3 0.0 copy-start.7
  0.3 0.6 copy-done.7
  1.0 0.7 %shard_map.46.shifted_ref = f32[8,16,1024]{2,1,0:T(8,128)S(1)} custom-call(s32[8]{0:T(128)S(1)} %copy-done.7, bf16[16,1024]{1,0:T(8,128)(2,1)S(1)} %convert_element_type.22.table_ref), custom_call_target="tpu_custom_call" | custom-call | tf_op jit(solution)/shard_map/pallas_call | solution.py:46
  1.7 0.0 copy-start.2
  1.7 0.8 %copy-done.2 = f32[8,16,1024]{2,1,0:T(8,128)} copy-done((f32[8,16,1024]{2,1,0:T(8,128)}, f32[8,16,1024]{2,1,0:T(8,128)S(1)}, u32[]{:S(2)}) %copy-start.2) | copy-done | bytes 524312
  2.5 1.9 %copy.16 = bf16[32,8,2,512]{3,1,2,0:T(8,128)(2,1)} copy(bf16[32,8,2,512]{3,2,1,0:T(2,128)(2,1)} %bitcast.12) | data formatting | bytes 1048576
  4.4 0.0 copy-done.10
  4.4 1.2 %reshape_reshape_squeeze.3.recorded_ref = bf16[8,32,1024]{2,1,0:T(8,128)(2,1)} reshape(bf16[1,256,2,512]{3,2,1,0:T(2,128)(2,1)S(1)} %copy-done.10) | data formatting | bytes 1048576 | tf_op jit(solution)/shard_map/reshape;reshape;squeeze | solution.py:321
  5.6 0.0 copy-done.9
  5.6 1.5 %fusion.6 = (bf16[1,256,1,1024]{3,2,1,0:T(2,128)(2,1)S(1)}, bf16[1,256,1,1024]{3,2,1,0:T(2,128)(2,1)S(1)}) fusion(bf16[1,256,2,1024]{3,2,1,0:T(2,128)(2,1)S(1)} %copy-done.9), kind=kLoop, calls=%fused_computation.16 | loop fusion | bytes 2097152 | tf_op jit(solution)/shard_map/slice | solution.py:334
  7.1 0.0 copy-start.3
  7.1 0.0 copy-start.5
  7.1 0.0 copy-start.6
  7.1 0.0 copy-start.8
  7.1 0.4 copy_bitcast_fusion
  7.5 0.6 copy-done.3
  8.1 0.2 copy-done.5
  8.3 0.2 copy-done.6
  8.4 0.0 copy-done.8
  8.4 33.4 %shard_map.47 = (bf16[8,32,1024]{2,1,0:T(8,128)(2,1)S(1)}, bf16[8,32,1024]{2,1,0:T(8,128)(2,1)S(1)}, bf16[8,16,128]{2,1,0:T(8,128)(2,1)S(1)}, bf16[32,48,1024]{2,1,0:T(8,128)(2,1)S(1)}) custom-call(f32[3,8,32]{2,1,0:T(8,128)S(1)} %copy-done.8, f32[8,16,1024]{2,1,0:T(8,128)S(1)} %copy-done.3, bf16[256,1024]{1,0:T(8,128)(2,1)S(1)} %get-tuple-element.20.real_ref, ...), custom_call_target="tpu_custom_call" | custom-call | flops 1073741824 | bytes 4718592 | tf_op jit(solution)/shard_map/pallas_call | solution.py:295
  41.9 0.0 copy-start.4
  41.9 0.8 %copy-done.4 = bf16[8,32,1024]{2,1,0:T(8,128)(2,1)} copy-done((bf16[8,32,1024]{2,1,0:T(8,128)(2,1)}, bf16[8,32,1024]{2,1,0:T(8,128)(2,1)S(1)}, u32[]{:S(2)}) %copy-start.4) | copy-done | bytes 524312
  42.7 1.1 %copy.12 = bf16[32,8,1024]{2,1,0:T(8,128)(2,1)} copy(bf16[32,8,1024]{2,0,1:T(8,128)(2,1)S(1)} %bitcast.11) | data formatting | bytes 1048576 | tf_op jit(solution)/shard_map/transpose | solution.py:342
  43.8 2.0 %reshape.118.recorded_ref = bf16[32,16,512]{2,1,0:T(8,128)(2,1)} reshape(bf16[32,8,1024]{2,1,0:T(8,128)(2,1)} %copy.12) | data formatting | bytes 1048576 | tf_op jit(solution)/shard_map/reshape | solution.py:342
  45.8 0.1 fusion.7
  45.9 1.3 %maximum_bitcast_fusion = bf16[34,8,1024]{2,0,1:T(8,128)(2,1)S(1)} fusion(bf16[8,1,1024]{2,1,0:T(2,128)(2,1)S(1)} %get-tuple-element.16, bf16[8,32,1024]{2,1,0:T(8,128)(2,1)} %copy-done.4, bf16[8,1,1024]{2,1,0:T(2,128)(2,1)S(1)} %get-tuple-element.15), kind=kLoop, calls=%fused_computation | loop fusion | flops 1671168 | bytes 1114112 | tf_op jit(solution)/shard_map/transpose | solution.py:342
  47.1 1.1 %copy.13 = bf16[34,8,1024]{2,1,0:T(8,128)(2,1)} copy(bf16[34,8,1024]{2,0,1:T(8,128)(2,1)S(1)} %maximum_bitcast_fusion) | data formatting | bytes 1114112 | tf_op jit(solution)/shard_map/transpose | solution.py:342
  48.3 2.0 %reshape.120.predicted_ref = bf16[34,16,512]{2,1,0:T(8,128)(2,1)} reshape(bf16[34,8,1024]{2,1,0:T(8,128)(2,1)} %copy.13) | data formatting | bytes 1114112 | tf_op jit(solution)/shard_map/reshape | solution.py:342
  50.3 1.1 %copy-done = bf16[34,16,512]{2,1,0:T(8,128)(2,1)S(1)} copy-done((bf16[34,16,512]{2,1,0:T(8,128)(2,1)S(1)}, bf16[34,16,512]{2,1,0:T(8,128)(2,1)}, u32[]{:S(2)}) %copy-start) | copy-done | bytes 557080
  51.3 1.0 %copy-done.1 = bf16[32,16,512]{2,1,0:T(8,128)(2,1)S(1)} copy-done((bf16[32,16,512]{2,1,0:T(8,128)(2,1)S(1)}, bf16[32,16,512]{2,1,0:T(8,128)(2,1)}, u32[]{:S(2)}) %copy-start.1) | copy-done | bytes 524312
  52.4 17.1 %shard_map.48 = bf16[32,512,1024]{2,1,0:T(8,128)(2,1)} custom-call(bf16[16,1024]{1,0:T(8,128)(2,1)S(1)} %convert_element_type.22.table_ref, bf16[32,48,1024]{2,1,0:T(8,128)(2,1)S(1)} %get-tuple-element.9.basis_ref, bf16[32,16,512]{2,1,0:T(8,128)(2,1)S(1)} %copy-done.1, bf16[34,16,512]{2,1,0:T(8,128)(2,1)S(1)} %copy-done), custom_call_target="tpu_custom_call" | custom-call | flops 2147483648 | bytes 33554432 | tf_op jit(solution)/shard_map/pallas_call | solution.py:100
  (9 shorter events, 0.1 us)
Async XLA Ops:
  0.3 0.7 copy-start.7
  1.0 3.4 %copy-start.10 = (bf16[1,256,2,512]{3,2,1,0:T(2,128)(2,1)S(1)}, bf16[1,256,2,512]{3,2,1,0:T(2,128)(2,1)}, u32[]{:S(2)}) copy-start(bf16[1,256,2,512]{3,2,1,0:T(2,128)(2,1)} %param.5) | copy-start | bytes 1572868
  1.0 4.6 %copy-start.9 = (bf16[1,256,2,1024]{3,2,1,0:T(2,128)(2,1)S(1)}, bf16[1,256,2,1024]{3,2,1,0:T(2,128)(2,1)}, u32[]{:S(2)}) copy-start(bf16[1,256,2,1024]{3,2,1,0:T(2,128)(2,1)} %param.4) | copy-start | bytes 3145732
  1.7 0.8 %copy-start.2 = (f32[8,16,1024]{2,1,0:T(8,128)}, f32[8,16,1024]{2,1,0:T(8,128)S(1)}, u32[]{:S(2)}) copy-start(f32[8,16,1024]{2,1,0:T(8,128)S(1)} %shard_map.46.shifted_ref) | copy-start | bytes 1572868
  7.1 1.0 %copy-start.3 = (f32[8,16,1024]{2,1,0:T(8,128)S(1)}, f32[8,16,1024]{2,1,0:T(8,128)}, u32[]{:S(2)}) copy-start(f32[8,16,1024]{2,1,0:T(8,128)} %copy-done.2) | copy-start | bytes 1572868
  7.1 1.2 %copy-start.5 = (bf16[32,8,2,512]{3,1,2,0:T(8,128)(2,1)S(1)}, bf16[32,8,2,512]{3,1,2,0:T(8,128)(2,1)}, u32[]{:S(2)}) copy-start(bf16[32,8,2,512]{3,1,2,0:T(8,128)(2,1)} %copy.16) | copy-start | bytes 1572868
  7.1 1.3 %copy-start.6 = (bf16[8,32,1024]{2,1,0:T(8,128)(2,1)S(1)}, bf16[8,32,1024]{2,1,0:T(8,128)(2,1)}, u32[]{:S(2)}) copy-start(bf16[8,32,1024]{2,1,0:T(8,128)(2,1)} %reshape_reshape_squeeze.3.recorded_ref) | copy-start | bytes 1572868
  7.1 1.3 %copy-start.8 = (f32[3,8,32]{2,1,0:T(8,128)S(1)}, f32[3,8,32]{2,1,0:T(8,128)}, u32[]{:S(2)}) copy-start(f32[3,8,32]{2,1,0:T(8,128)} %weights_ref.1) | copy-start | bytes 9220
  41.9 0.8 %copy-start.4 = (bf16[8,32,1024]{2,1,0:T(8,128)(2,1)}, bf16[8,32,1024]{2,1,0:T(8,128)(2,1)S(1)}, u32[]{:S(2)}) copy-start(bf16[8,32,1024]{2,1,0:T(8,128)(2,1)S(1)} %get-tuple-element.12) | copy-start | bytes 1572868
  50.3 1.1 %copy-start = (bf16[34,16,512]{2,1,0:T(8,128)(2,1)S(1)}, bf16[34,16,512]{2,1,0:T(8,128)(2,1)}, u32[]{:S(2)}) copy-start(bf16[34,16,512]{2,1,0:T(8,128)(2,1)} %reshape.120.predicted_ref) | copy-start | bytes 1671172
  51.3 1.0 %copy-start.1 = (bf16[32,16,512]{2,1,0:T(8,128)(2,1)S(1)}, bf16[32,16,512]{2,1,0:T(8,128)(2,1)}, u32[]{:S(2)}) copy-start(bf16[32,16,512]{2,1,0:T(8,128)(2,1)} %reshape.118.recorded_ref) | copy-start | bytes 1572868
